TPU v7x, 32 devices: a whole 2x2x4 slice. The times are simulated.
32 devices in a mesh: dp: 8 (over z, y), nbr: 4 (over x, core).
Axes of the slice: x: 2, y: 2, z: 4, core: 2. Of those that a mesh axis runs over, the one named last changes fastest.
Arguments:
- queries: bfloat16 [6144, 4096], P(('dp', 'nbr')), may hold values from -256 to 256
- cotangent: bfloat16 [6144, 4096], P(('dp', 'nbr')), may hold values from -1 to 1
- pool: bfloat16 [64, 128, 896], P('dp', 'nbr'), may hold values from -60 to 60
- enc_gain: float32 [896], replicated, may hold values from 0.25 to 1.75
- enc_weight: bfloat16 [896, 896], replicated, may hold values from -0.1875 to 0.1875
- k_weight: bfloat16 [896, 4096], P(None, 'nbr'), may hold values from -0.1875 to 0.1875
- v_weight: bfloat16 [896, 4096], P(None, 'nbr'), may hold values from -0.1875 to 0.1875
- nbr_owner: int32 [96, 1], replicated, may hold values from 0 to 7; in each aligned block of 12 rows (0 to 11, 12 to 23, ...) at most 2 rows name the same one
- nbr_slot: int32 [96, 1], replicated, may hold values from 0 to 7
Outputs:
- attended: bfloat16 [6144, 4096], P(('dp', 'nbr'))
- grad_k: float32 [896, 4096], P('dp', 'nbr')
- grad_v: float32 [896, 4096], P('dp', 'nbr')
Inputs may be any that keep to these rules, and one draw needn't show every extreme that they name: `nbr_owner`: within the 12 groups of one sequence at most 2 name the same index of dp, and this bound is reached.
All inputs are finite; a program needn't handle non-finite values.
Results may differ from a plain program's by a relative error of at most 0.035.
The roundings to bfloat16 on the way count: a program that leaves them out, or rounds other values in their place, can miss the bound.
Values may be sent and summed in bfloat16 or wider, within the bound.
A program may use at most 128 MiB of HBM per device.

v0:
```python
import jax
import jax.numpy as jnp
from jax import lax
from jax.experimental import pallas as pl
from jax.experimental.pallas import tpu as pltpu
from jax.sharding import PartitionSpec as P

HEAD = 128
GROUP = 64
CAP = 2
BF = jnp.bfloat16
F32 = jnp.float32


def encode(blocks, gain_vec, weight):
    widened = blocks.astype(F32)
    mean_sq = jnp.mean(widened * widened, axis=-1, keepdims=True)
    normed = (widened * lax.rsqrt(mean_sq + 1e-06) * gain_vec).astype(BF)
    combined = jnp.dot(normed, weight, preferred_element_type=F32)
    return (widened + jax.nn.gelu(combined)).astype(BF)


def pick_rows(chosen, rows, tokens):
    m, n = chosen.shape
    eye = jnp.eye(tokens, dtype=BF)
    full = chosen.astype(BF)[:, None, :, None] * eye[None, :, None, :]
    full = full.reshape(m * tokens, n * tokens)
    return jnp.dot(full, rows, preferred_element_type=F32).astype(BF)


def attention_body(q_ref, g_ref, k_ref, v_ref, o_ref, dk_ref, dv_ref):
    heads = q_ref.shape[1] // HEAD
    parts, _, tokens, _ = k_ref.shape
    keys = parts * tokens
    scale = HEAD ** (-0.5)
    over_last = (((1,), (1,)), ((), ()))
    over_first = (((0,), (0,)), ((), ()))
    for first in range(0, heads, 4):
        held = []
        for h in range(first, min(first + 4, heads)):
            cols = slice(h * HEAD, (h + 1) * HEAD)
            k = k_ref[:, 0, :, cols].reshape(keys, HEAD)
            v = v_ref[:, 0, :, cols].reshape(keys, HEAD)
            s = lax.dot_general(q_ref[:, cols], k, over_last, preferred_element_type=F32)
            dw = lax.dot_general(g_ref[:, cols], v, over_last, preferred_element_type=F32)
            held.append((cols, v, s * scale, dw.astype(BF).astype(F32)))
        ready = []
        for cols, v, s, dw in held:
            e = jnp.exp(s - jnp.max(s, axis=-1, keepdims=True))
            p = e * (1.0 / jnp.sum(e, axis=-1, keepdims=True))
            ds = p * (dw - jnp.sum(dw * p, axis=-1, keepdims=True)) * scale
            ready.append((cols, v, p.astype(BF), ds.astype(BF)))
        for cols, v, w, ds in ready:
            q, g = q_ref[:, cols], g_ref[:, cols]
            o_ref[:, cols] = jnp.dot(w, v, preferred_element_type=F32).astype(BF)
            dk = lax.dot_general(ds, q, over_first, preferred_element_type=F32)
            dv = lax.dot_general(w, g, over_first, preferred_element_type=F32)
            dk_ref[:, 0, :, cols] = dk.astype(BF).reshape(parts, tokens, HEAD)
            dv_ref[:, 0, :, cols] = dv.astype(BF).reshape(parts, tokens, HEAD)


def attention(q, g, k, v):
    length, width = q.shape
    parts, groups, tokens, _ = k.shape
    row = pl.BlockSpec((GROUP, width), lambda c: (c, 0))
    block = pl.BlockSpec((parts, 1, tokens, width), lambda c: (0, c, 0, 0))
    work = 10 * length * parts * tokens * width
    return pl.pallas_call(
        attention_body,
        grid=(groups,),
        in_specs=[row, row, block, block],
        out_specs=[row, block, block],
        out_shape=[
            jax.ShapeDtypeStruct(q.shape, BF),
            jax.ShapeDtypeStruct(k.shape, BF),
            jax.ShapeDtypeStruct(v.shape, BF),
        ],
        compiler_params=pltpu.CompilerParams(vmem_limit_bytes=32 * 2**20),
        cost_estimate=pl.CostEstimate(
            flops=work,
            bytes_accessed=6 * length * width + 8 * k.size,
            transcendentals=length * parts * tokens * width // HEAD,
        ),
    )(q, g, k, v)


def exchange(x, axis, split, join):
    n = lax.axis_size(axis)
    me = lax.axis_index(axis)
    span = x.shape[split] // n
    step = x.shape[join]
    parts = []
    for d in range(n):
        piece = lax.dynamic_slice_in_dim(x, (me ^ d) * span, span, split)
        if d:
            piece = lax.ppermute(piece, axis, [(i, i ^ d) for i in range(n)])
        parts.append(piece)
    shape = list(parts[0].shape)
    shape[join] = n * step
    whole = jnp.zeros(shape, x.dtype)
    for d, piece in enumerate(parts):
        whole = lax.dynamic_update_slice_in_dim(whole, piece, (me ^ d) * step, join)
    return whole


def halving(total, axis, turn):
    n = lax.axis_size(axis)
    me = lax.axis_index(axis)
    count = n.bit_length() - 1
    bits = [(i + turn) % count for i in range(count)]
    rows, width = total.shape
    current = total.reshape((2,) * count + (rows // n, width))
    left = list(range(count - 1, -1, -1))
    for bit in bits:
        place = left.index(bit)
        left.pop(place)
        mine = (me >> bit) & 1
        away = lax.dynamic_index_in_dim(current, 1 - mine, place, keepdims=False)
        keep = lax.dynamic_index_in_dim(current, mine, place, keepdims=False)
        pairs = [(i, i ^ (1 << bit)) for i in range(n)]
        current = keep + lax.ppermute(away.astype(BF), axis, pairs).astype(F32)
    return current


def per_device(
    queries, cotangent, pool, enc_gain, enc_weight, k_weight, v_weight, nbr_owner, nbr_slot
):
    dp_count = lax.axis_size("dp")
    nbr_count = lax.axis_size("nbr")
    me = lax.axis_index("dp")
    held, tokens, enc_width = pool.shape
    per_row = nbr_owner.shape[0] // dp_count

    owners = nbr_owner[:, 0].reshape(dp_count, per_row)
    slots = nbr_slot[:, 0].reshape(dp_count, per_row)
    same = owners[:, :, None] == owners[:, None, :]
    earlier = jnp.tril(jnp.ones((per_row, per_row), jnp.bool_), -1)
    rank = jnp.sum((same & earlier[None]).astype(jnp.int32), axis=-1)

    ranks = jnp.arange(CAP, dtype=jnp.int32)
    blocks = jnp.arange(held, dtype=jnp.int32)
    mine = (owners == me)[:, None, :] & (rank[:, None, :] == ranks[None, :, None])
    send = jnp.any(
        mine[:, :, None, :] & (slots[:, None, None, :] == blocks[None, None, :, None]), axis=-1
    ).reshape(dp_count * CAP, held)
    enc = encode(pool.reshape(held * tokens, enc_width), enc_gain, enc_weight)
    outgoing = pick_rows(send, enc, tokens)
    arrived = lax.all_to_all(outgoing, "dp", split_axis=0, concat_axis=0, tiled=True)

    q_rows = exchange(queries, "nbr", 1, 0)
    arrived, q_rows = lax.optimization_barrier((arrived, q_rows))

    place = lax.dynamic_slice_in_dim(owners * CAP + rank, me, 1, 0)[0]
    take = place[:, None] == jnp.arange(dp_count * CAP, dtype=jnp.int32)[None, :]
    picked = pick_rows(take, arrived, tokens)
    flat_enc = lax.all_gather(picked, "nbr", axis=0, tiled=True)

    g_rows = exchange(cotangent, "nbr", 1, 0)
    seq_len, width = q_rows.shape
    lead = GROUP - 1
    blank = jnp.zeros((lead, width), BF)
    q_rows = jnp.concatenate([q_rows[lead:], blank], axis=0)
    g_rows = jnp.concatenate([g_rows[lead:], blank], axis=0)

    shape4 = (nbr_count, per_row, tokens, width)
    keys = jnp.dot(flat_enc, k_weight, preferred_element_type=F32).astype(BF)
    values = jnp.dot(flat_enc, v_weight, preferred_element_type=F32).astype(BF)
    out, dk, dv = attention(q_rows, g_rows, keys.reshape(shape4), values.reshape(shape4))

    over_first = (((0,), (0,)), ((), ()))

    def weight_grad(grads):
        return lax.dot_general(
            flat_enc, grads.reshape(-1, width), over_first, preferred_element_type=F32
        )

    grad_v = halving(weight_grad(dv), "dp", 0)
    product_k = weight_grad(dk)
    cut = width // HEAD * 3 // 8 * HEAD
    grad_k = jnp.concatenate(
        [halving(product_k[:, :cut], "dp", 0), halving(product_k[:, cut:], "dp", 1)], axis=1
    )
    out = jnp.concatenate([blank, out[: seq_len - lead]], axis=0)
    merged = exchange(out, "nbr", 0, 1)
    return (merged, grad_k, grad_v)


def solution(mesh):
    return jax.shard_map(
        per_device,
        mesh=mesh,
        in_specs=(
            P(("dp", "nbr"), None),
            P(("dp", "nbr"), None),
            P("dp", "nbr", None),
            P(),
            P(),
            P(None, "nbr"),
            P(None, "nbr"),
            P(),
            P(),
        ),
        out_specs=(P(("dp", "nbr"), None), P("dp", "nbr"), P("dp", "nbr")),
        check_vma=False,
    )
```

profile of v0, /device:TPU:0, one launch (start us, length us, event | category | flops | bytes accessed | tf_op | source)
XLA Modules:
  0.0 200.0 jit_solution(11932165146659722679)
XLA Ops:
  7.2 0.5 broadcast.81
  7.7 1.3 reduce.10
  9.3 0.4 convert_reduce_fusion
  9.8 1.3 reduce.9
  11.2 0.4 and_reduce_fusion
  11.7 1.4 mul.124
  13.4 0.2 fusion.12
  13.6 2.3 %fusion.8 = bf16[256,896]{1,0:T(8,128)(2,1)S(1)} fusion(bf16[8,32,896]{2,1,0:T(8,128)(2,1)S(1)} %copy-done.5, bf16[256,896]{1,0:T(8,128)(2,1)S(1)} %fusion.12, bf16[896,896]{1,0:T(8,128)(2,1)} %param.13), kind=kOutput, calls=%fused_computation.21 | convolution fusion | flops 413564928 | bytes 2981888 | tf_op jit(solution)/shard_map/dot_general | solution.py:19
  15.9 1.4 convolution_convert_fusion.2
  17.3 7.4 %all-to-all-start = ((bf16[8,64,896]{2,1,0:T(8,128)(2,1)}), bf16[8,64,896]{2,1,0:T(8,128)(2,1)}, u32[]{:S(2)}, u32[]{:S(2)}) async-start(bf16[8,64,896]{2,1,0:T(8,128)(2,1)} %bitcast.2), calls=%async_computation | async-start | bytes 1835008 | tf_op jit(solution)/shard_map/all_to_all | solution.py:148
  24.8 1.3 broadcast.73.clone
  26.1 1.2 constant_dynamic-slice_fusion.7
  27.3 1.5 collective-permute-start.1
  28.8 0.4 collective-permute-start.2
  29.1 0.2 fusion.25
  29.4 0.2 broadcast_multiply_fusion
  29.6 2.4 %mul.150 = bf16[384,512]{1,0:T(8,128)(2,1)} reshape(bf16[12,32,16,32]{3,2,1,0:T(8,128)(2,1)S(1)} %broadcast_multiply_fusion) | data formatting | bytes 786432 | tf_op jit(solution)/shard_map/mul | solution.py:26
  32.0 1.8 constant_dynamic-update-slice_fusion.8
  33.8 5.7 %collective-permute-done.1 = bf16[192,1024]{1,0:T(8,128)(2,1)} collective-permute-done((bf16[192,1024]{1,0:T(8,128)(2,1)}, bf16[192,1024]{1,0:T(8,128)(2,1)}, u32[]{:S(2)}, u32[]{:S(2)}) %collective-permute-start.1) | collective-permute-done | bytes 393248 | tf_op jit(solution)/shard_map/ppermute | solution.py:96
  39.5 1.8 constant_dynamic-update-slice_fusion.7
  41.3 5.9 %collective-permute-done.2 = bf16[192,1024]{1,0:T(8,128)(2,1)} collective-permute-done((bf16[192,1024]{1,0:T(8,128)(2,1)}, bf16[192,1024]{1,0:T(8,128)(2,1)}, u32[]{:S(2)}, u32[]{:S(2)}) %collective-permute-start.2) | collective-permute-done | bytes 393248 | tf_op jit(solution)/shard_map/ppermute | solution.py:96
  47.2 1.8 constant_dynamic-update-slice_fusion.6
  48.9 2.6 %convolution_convert_fusion.3 = bf16[384,896]{1,0:T(8,128)(2,1)} fusion(bf16[384,512]{1,0:T(8,128)(2,1)S(1)} %copy-done.8, bf16[512,896]{1,0:T(8,128)(2,1)} %bitcast.3), kind=kOutput, calls=%fused_computation.6 | convolution fusion | flops 352665600 | bytes 1998848 | tf_op jit(solution)/shard_map/dot_general | solution.py:28
  51.6 0.2 broadcast.73.clone.1
  51.8 2.4 %constant_dynamic-slice_fusion.3 = (bf16[192,1024]{1,0:T(8,128)(2,1)}, bf16[192,1024]{1,0:T(8,128)(2,1)}, bf16[768,1024]{1,0:T(8,128)(2,1)S(1)}, bf16[192,1024]{1,0:T(8,128)(2,1)}) fusion(bf16[192,4096]{1,0:T(8,128)(2,1)} %param.10, s32[]{:T(128)S(6)} %select_n.90, s32[]{:T(128)S(6)} %select_n.86, bf16[768,1024]{1,0:T(8,128)(2,1)S(1)} %broadcast.73.clone.1, ...), kind=kLoop, calls=%fused_computation.69 | loop fusion | bytes 3145748 | tf_op jit(solution)/shard_map/dynamic_slice | solution.py:94
  54.2 0.5 collective-permute-start.3
  54.7 1.5 collective-permute-start.4
  56.2 0.2 collective-permute-done.3
  56.4 1.0 constant_dynamic-update-slice_fusion.5
  57.4 13.4 %collective-permute-done.4 = bf16[192,1024]{1,0:T(8,128)(2,1)} collective-permute-done((bf16[192,1024]{1,0:T(8,128)(2,1)}, bf16[192,1024]{1,0:T(8,128)(2,1)}, u32[]{:S(2)}, u32[]{:S(2)}) %collective-permute-start.4) | collective-permute-done | bytes 393248 | tf_op jit(solution)/shard_map/ppermute | solution.py:96
  70.8 1.0 constant_dynamic-update-slice_fusion.4
  71.9 14.9 %collective-permute-done.5 = bf16[192,1024]{1,0:T(8,128)(2,1)} collective-permute-done((bf16[192,1024]{1,0:T(8,128)(2,1)}, bf16[192,1024]{1,0:T(8,128)(2,1)}, u32[]{:S(2)}, u32[]{:S(2)}) %collective-permute-start.5) | collective-permute-done | bytes 393248 | tf_op jit(solution)/shard_map/ppermute | solution.py:96
  86.7 1.0 constant_dynamic-update-slice_fusion.3
  87.8 0.3 slice.20
  88.3 1.7 slice.15
  90.0 1.3 concatenate.12.q_ref
  91.3 4.6 %copy.33 = bf16[896,1536]{1,0:T(8,128)(2,1)} copy(bf16[896,1536]{0,1:T(8,128)(2,1)} %bitcast.90) | data formatting | bytes 5505024 | tf_op jit(solution)/shard_map/dot_general | solution.py:173
  95.9 5.6 %convolution_convert_fusion.1 = bf16[1536,1024]{1,0:T(8,128)(2,1)S(1)} fusion(bf16[1536,896]{1,0:T(8,128)(2,1)} %all-gather.2.cloned.1.call-done, bf16[896,1024]{1,0:T(8,128)(2,1)S(1)} %copy-done), kind=kOutput, calls=%fused_computation.1 | convolution fusion | flops 2820145152 | bytes 7733248 | tf_op jit(solution)/shard_map/dot_general | solution.py:166
  101.5 3.7 %convolution_convert_fusion = bf16[1536,1024]{1,0:T(8,128)(2,1)S(1)} fusion(bf16[1536,896]{1,0:T(8,128)(2,1)S(1)} %copy-done.3, bf16[896,1024]{1,0:T(8,128)(2,1)S(1)} %copy-done.11), kind=kOutput, calls=%fused_computation | convolution fusion | flops 2820145152 | bytes 7733248 | tf_op jit(solution)/shard_map/dot_general | solution.py:167
  105.2 17.7 %shard_map.112 = (bf16[768,1024]{1,0:T(8,128)(2,1)S(1)}, bf16[4,12,32,1024]{3,2,1,0:T(8,128)(2,1)S(1)}, bf16[4,12,32,1024]{3,2,1,0:T(8,128)(2,1)S(1)}) custom-call(bf16[768,1024]{1,0:T(8,128)(2,1)S(1)} %copy-done.2, bf16[768,1024]{1,0:T(8,128)(2,1)S(1)} %concatenate.13.g_ref, bf16[4,12,32,1024]{3,2,1,0:T(8,128)(2,1)S(1)} %bitcast.82, ...), custom_call_target="tpu_custom_call" | custom-call | flops 1006632960 | bytes 17301504 | tf_op jit(solution)/shard_map/pallas_call | solution.py:68
  123.0 3.1 %fusion.27 = f32[896,1024]{1,0:T(8,128)S(1)} fusion(bf16[1536,896]{1,0:T(8,128)(2,1)S(1)} %copy-done.3, bf16[1536,1024]{1,0:T(8,128)(2,1)S(1)} %bitcast.85), kind=kOutput, calls=%fused_computation.90 | convolution fusion | flops 2818572288 | bytes 9568256 | tf_op jit(solution)/shard_map/dot_general | solution.py:173
  126.3 1.9 collective-permute-start.9
  128.2 3.0 %fusion.28 = f32[2,2,2,112,1024]{4,3,2,1,0:T(8,128)S(1)} fusion(bf16[2,2,2,112,1536]{4,3,2,1,0:T(8,128)(2,1)S(1)} %bitcast.91, bf16[1536,1024,1,1,1]{1,0,4,3,2:T(8,128)(2,1)S(1)} %bitcast.84), kind=kOutput, calls=%fused_computation.91 | convolution fusion | flops 2818572288 | bytes 9568256 | tf_op jit(solution)/shard_map/dot_general | solution.py:173
  131.4 0.2 slice.22
  131.6 1.6 collective-permute-start.15
  133.3 0.2 broadcast_in_dim.3
  133.4 1.2 pad_dynamic-slice_fusion
  134.8 1.5 collective-permute-start.12
  136.3 2.3 %collective-permute-start.7 = (bf16[192,1024]{1,0:T(8,128)(2,1)S(1)}, bf16[192,1024]{1,0:T(8,128)(2,1)S(1)}, u32[]{:S(2)}, u32[]{:S(2)}) collective-permute-start(bf16[192,1024]{1,0:T(8,128)(2,1)S(1)} %get-tuple-element.23), channel_id=1, source_target_pairs={{0,2},{1,3},{2,0},{3,1},{4,6},{5,7},{6,4},{7,5},{8,10},{9,11},{10,... | collective-permute-start | bytes 1179656 | tf_op jit(solution)/shard_map/ppermute | solution.py:96
  138.9 1.8 collective-permute-start.10
  140.7 7.9 %collective-permute-done.7 = bf16[192,1024]{1,0:T(8,128)(2,1)S(1)} collective-permute-done((bf16[192,1024]{1,0:T(8,128)(2,1)S(1)}, bf16[192,1024]{1,0:T(8,128)(2,1)S(1)}, u32[]{:S(2)}, u32[]{:S(2)}) %collective-permute-start.7) | collective-permute-done | bytes 393248 | tf_op jit(solution)/shard_map/ppermute | solution.py:96
  148.6 6.7 %collective-permute-done.8 = bf16[192,1024]{1,0:T(8,128)(2,1)S(1)} collective-permute-done((bf16[192,1024]{1,0:T(8,128)(2,1)S(1)}, bf16[192,1024]{1,0:T(8,128)(2,1)S(1)}, u32[]{:S(2)}, u32[]{:S(2)}) %collective-permute-start.8) | collective-permute-done | bytes 393248 | tf_op jit(solution)/shard_map/ppermute | solution.py:96
  155.5 2.4 %collective-permute-start.11 = (bf16[112,384]{1,0:T(8,128)(2,1)S(1)}, bf16[112,384]{1,0:T(8,128)(2,1)S(1)}, u32[]{:S(2)}, u32[]{:S(2)}) collective-permute-start(bf16[112,384]{1,0:T(8,128)(2,1)S(1)} %fusion.21), channel_id=1, source_target_pairs={{0,16},{4,20},{8,24},{12,28},{16,0},{20,4},{24,8},{28,12},{1,17},{... | collective-permute-start | bytes 258056 | tf_op jit(solution)/shard_map/ppermute | solution.py:121
  158.0 0.9 collective-permute-start.13
  158.9 0.4 bitcast_add_fusion
  159.4 0.6 collective-permute-start.16
  160.1 9.8 %collective-permute-done.11 = bf16[112,384]{1,0:T(8,128)(2,1)S(1)} collective-permute-done((bf16[112,384]{1,0:T(8,128)(2,1)S(1)}, bf16[112,384]{1,0:T(8,128)(2,1)S(1)}, u32[]{:S(2)}, u32[]{:S(2)}) %collective-permute-start.11) | collective-permute-done | bytes 86048 | tf_op jit(solution)/shard_map/ppermute | solution.py:121
  169.9 6.0 %collective-permute-done.13 = bf16[2,112,640]{2,1,0:T(8,128)(2,1)S(1)} collective-permute-done((bf16[2,112,640]{2,1,0:T(8,128)(2,1)S(1)}, bf16[2,112,640]{2,1,0:T(8,128)(2,1)S(1)}, u32[]{:S(2)}, u32[]{:S(2)}) %collective-permute-start.13) | collective-permute-done | bytes 286752 | tf_op jit(solution)/shard_map/ppermute | solution.py:121
  176.0 0.5 collective-permute-start.14
  176.5 3.4 %collective-permute-done.16 = bf16[2,112,1024]{2,1,0:T(8,128)(2,1)S(1)} collective-permute-done((bf16[2,112,1024]{2,1,0:T(8,128)(2,1)S(1)}, bf16[2,112,1024]{2,1,0:T(8,128)(2,1)S(1)}, u32[]{:S(2)}, u32[]{:S(2)}) %collective-permute-start.16) | collective-permute-done | bytes 458784 | tf_op jit(solution)/shard_map/ppermute | solution.py:121
  180.3 1.5 collective-permute-done.14
  181.8 0.8 pad_maximum_fusion
  182.6 9.8 %collective-permute-done.17 = bf16[112,1024]{1,0:T(8,128)(2,1)S(1)} collective-permute-done((bf16[112,1024]{1,0:T(8,128)(2,1)S(1)}, bf16[112,1024]{1,0:T(8,128)(2,1)S(1)}, u32[]{:S(2)}, u32[]{:S(2)}) %collective-permute-start.17) | collective-permute-done | bytes 229408 | tf_op jit(solution)/shard_map/ppermute | solution.py:121
  192.4 0.8 bitcast_add_fusion.5
  (77 shorter events, 2.8 us)
Async XLA Ops:
  7.2 88.7 %copy-start = (bf16[896,1024]{1,0:T(8,128)(2,1)S(1)}, bf16[896,1024]{1,0:T(8,128)(2,1)}, u32[]{:S(2)}) copy-start(bf16[896,1024]{1,0:T(8,128)(2,1)} %param.14) | copy-start | bytes 5505028
  7.2 6.0 %copy-start.5 = (bf16[8,32,896]{2,1,0:T(8,128)(2,1)S(1)}, bf16[8,32,896]{2,1,0:T(8,128)(2,1)}, u32[]{:S(2)}) copy-start(bf16[8,32,896]{2,1,0:T(8,128)(2,1)} %param.11) | copy-start | bytes 1376260
  7.2 6.2 %copy-start.10 = (f32[896]{0:T(1024)S(1)}, f32[896]{0:T(1024)}, u32[]{:S(2)}) copy-start(f32[896]{0:T(1024)} %param.12) | copy-start | bytes 10756
  13.6 2.3 %copy-start.9 = (bf16[512,256]{1,0:T(8,128)(2,1)S(1)}, bf16[512,256]{1,0:T(8,128)(2,1)}, u32[]{:S(2)}) copy-start(bf16[512,256]{1,0:T(8,128)(2,1)} %mul.124) | copy-start | bytes 786436
  17.3 8.8 %copy-start.6 = (bf16[192,4096]{1,0:T(8,128)(2,1)S(1)}, bf16[192,4096]{1,0:T(8,128)(2,1)}, u32[]{:S(2)}) copy-start(bf16[192,4096]{1,0:T(8,128)(2,1)} %param.9) | copy-start | bytes 4718596
  17.3 31.6 %all-to-all-start = ((bf16[8,64,896]{2,1,0:T(8,128)(2,1)}), bf16[8,64,896]{2,1,0:T(8,128)(2,1)}, u32[]{:S(2)}, u32[]{:S(2)}) async-start(bf16[8,64,896]{2,1,0:T(8,128)(2,1)} %bitcast.2), calls=%async_computation | async-start | bytes 1835008 | tf_op jit(solution)/shard_map/all_to_all | solution.py:148
  24.7 66.5 %all-gather.2.cloned.1.call-start = ((), (), s32[]{:S(2)}) async-start(), calls=%async_computation.1 | async-start | bytes 3440640 | tf_op jit(solution)/shard_map/all_gather | solution.py:156
  27.3 4.7 %collective-permute-start = (bf16[192,1024]{1,0:T(8,128)(2,1)}, bf16[192,1024]{1,0:T(8,128)(2,1)}, u32[]{:S(2)}, u32[]{:S(2)}) collective-permute-start(bf16[192,1024]{1,0:T(8,128)(2,1)} %get-tuple-element.18), channel_id=1, source_target_pairs={{0,1},{1,0},{2,3},{3,2},{4,5},{5,4},{6,7},{7,6},{8,9},{9,8},{10,11... | collective-permute-start | bytes 1179656 | tf_op jit(solution)/shard_map/ppermute | solution.py:96
  27.3 12.2 %collective-permute-start.1 = (bf16[192,1024]{1,0:T(8,128)(2,1)}, bf16[192,1024]{1,0:T(8,128)(2,1)}, u32[]{:S(2)}, u32[]{:S(2)}) collective-permute-start(bf16[192,1024]{1,0:T(8,128)(2,1)} %get-tuple-element.20), channel_id=1, source_target_pairs={{0,2},{1,3},{2,0},{3,1},{4,6},{5,7},{6,4},{7,5},{8,10},{9,11},{10,... | collective-permute-start | bytes 1179656 | tf_op jit(solution)/shard_map/ppermute | solution.py:96
  28.8 18.4 %collective-permute-start.2 = (bf16[192,1024]{1,0:T(8,128)(2,1)}, bf16[192,1024]{1,0:T(8,128)(2,1)}, u32[]{:S(2)}, u32[]{:S(2)}) collective-permute-start(bf16[192,1024]{1,0:T(8,128)(2,1)} %get-tuple-element.17), channel_id=1, source_target_pairs={{0,3},{1,2},{2,1},{3,0},{4,7},{5,6},{6,5},{7,4},{8,11},{9,10},{10,... | collective-permute-start | bytes 1179656 | tf_op jit(solution)/shard_map/ppermute | solution.py:96
  32.0 17.0 %copy-start.8 = (bf16[384,512]{1,0:T(8,128)(2,1)S(1)}, bf16[384,512]{1,0:T(8,128)(2,1)}, u32[]{:S(2)}) copy-start(bf16[384,512]{1,0:T(8,128)(2,1)} %mul.150) | copy-start | bytes 1179652
  54.2 2.2 %collective-permute-start.3 = (bf16[192,1024]{1,0:T(8,128)(2,1)}, bf16[192,1024]{1,0:T(8,128)(2,1)}, u32[]{:S(2)}, u32[]{:S(2)}) collective-permute-start(bf16[192,1024]{1,0:T(8,128)(2,1)} %get-tuple-element.14), channel_id=1, source_target_pairs={{0,1},{1,0},{2,3},{3,2},{4,5},{5,4},{6,7},{7,6},{8,9},{9,8},{10,11... | collective-permute-start | bytes 1179656 | tf_op jit(solution)/shard_map/ppermute | solution.py:96
  54.7 16.2 %collective-permute-start.4 = (bf16[192,1024]{1,0:T(8,128)(2,1)}, bf16[192,1024]{1,0:T(8,128)(2,1)}, u32[]{:S(2)}, u32[]{:S(2)}) collective-permute-start(bf16[192,1024]{1,0:T(8,128)(2,1)} %get-tuple-element.16), channel_id=1, source_target_pairs={{0,2},{1,3},{2,0},{3,1},{4,6},{5,7},{6,4},{7,5},{8,10},{9,11},{10,... | collective-permute-start | bytes 1179656 | tf_op jit(solution)/shard_map/ppermute | solution.py:96
  56.2 30.6 %collective-permute-start.5 = (bf16[192,1024]{1,0:T(8,128)(2,1)}, bf16[192,1024]{1,0:T(8,128)(2,1)}, u32[]{:S(2)}, u32[]{:S(2)}) collective-permute-start(bf16[192,1024]{1,0:T(8,128)(2,1)} %get-tuple-element.13), channel_id=1, source_target_pairs={{0,3},{1,2},{2,1},{3,0},{4,7},{5,6},{6,5},{7,4},{8,11},{9,10},{10,... | collective-permute-start | bytes 1179656 | tf_op jit(solution)/shard_map/ppermute | solution.py:96
  95.9 5.6 %copy-start.3 = (bf16[1536,896]{1,0:T(8,128)(2,1)S(1)}, bf16[1536,896]{1,0:T(8,128)(2,1)}, u32[]{:S(2)}) copy-start(bf16[1536,896]{1,0:T(8,128)(2,1)} %all-gather.2.cloned.1.call-done) | copy-start | bytes 8257540
  95.9 5.6 %copy-start.11 = (bf16[896,1024]{1,0:T(8,128)(2,1)S(1)}, bf16[896,1024]{1,0:T(8,128)(2,1)}, u32[]{:S(2)}) copy-start(bf16[896,1024]{1,0:T(8,128)(2,1)} %param.15) | copy-start | bytes 5505028
  101.5 3.7 %copy-start.2 = (bf16[768,1024]{1,0:T(8,128)(2,1)S(1)}, bf16[768,1024]{1,0:T(8,128)(2,1)}, u32[]{:S(2)}) copy-start(bf16[768,1024]{1,0:T(8,128)(2,1)} %concatenate.12.q_ref) | copy-start | bytes 4718596
  126.1 2.1 %copy-start.4 = (bf16[896,1536]{1,0:T(8,128)(2,1)S(1)}, bf16[896,1536]{1,0:T(8,128)(2,1)}, u32[]{:S(2)}) copy-start(bf16[896,1536]{1,0:T(8,128)(2,1)} %copy.33) | copy-start | bytes 8257540
  126.3 12.3 %collective-permute-start.9 = (bf16[2,2,112,384]{3,2,0,1:T(8,128)(2,1)S(1)}, bf16[2,2,112,384]{3,2,0,1:T(8,128)(2,1)S(1)}, u32[]{:S(2)}, u32[]{:S(2)}) collective-permute-start(bf16[2,2,112,384]{3,2,0,1:T(8,128)(2,1)S(1)} %fusion.16), channel_id=1, source_target_pairs={{0,4},{4,0},{8,12},{12,8},{16,20},{20,16},{24,28},{28,24},{1,5},{5... | collective-permute-start | bytes 1032200 | tf_op jit(solution)/shard_map/ppermute | solution.py:121
  131.6 27.3 %collective-permute-start.15 = (bf16[2,2,112,1024]{3,2,1,0:T(8,128)(2,1)S(1)}, bf16[2,2,112,1024]{3,2,1,0:T(8,128)(2,1)S(1)}, u32[]{:S(2)}, u32[]{:S(2)}) collective-permute-start(bf16[2,2,112,1024]{3,2,1,0:T(8,128)(2,1)S(1)} %fusion.9), channel_id=1, source_target_pairs={{0,4},{4,0},{8,12},{12,8},{16,20},{20,16},{24,28},{28,24},{1,5},{5... | collective-permute-start | bytes 2752520 | tf_op jit(solution)/shard_map/ppermute | solution.py:121
  134.6 4.3 %collective-permute-start.6 = (bf16[192,1024]{1,0:T(8,128)(2,1)S(1)}, bf16[192,1024]{1,0:T(8,128)(2,1)S(1)}, u32[]{:S(2)}, u32[]{:S(2)}) collective-permute-start(bf16[192,1024]{1,0:T(8,128)(2,1)S(1)} %get-tuple-element.22), channel_id=1, source_target_pairs={{0,1},{1,0},{2,3},{3,2},{4,5},{5,4},{6,7},{7,6},{8,9},{9,8},{10,11... | collective-permute-start | bytes 1179656 | tf_op jit(solution)/shard_map/ppermute | solution.py:96
  134.8 23.1 %collective-permute-start.12 = (bf16[2,2,112,640]{3,2,1,0:T(8,128)(2,1)S(1)}, bf16[2,2,112,640]{3,2,1,0:T(8,128)(2,1)S(1)}, u32[]{:S(2)}, u32[]{:S(2)}) collective-permute-start(bf16[2,2,112,640]{3,2,1,0:T(8,128)(2,1)S(1)} %fusion.13), channel_id=1, source_target_pairs={{0,8},{4,12},{8,0},{12,4},{16,24},{20,28},{24,16},{28,20},{1,9},{5... | collective-permute-start | bytes 1720328 | tf_op jit(solution)/shard_map/ppermute | solution.py:121
  136.3 12.3 %collective-permute-start.7 = (bf16[192,1024]{1,0:T(8,128)(2,1)S(1)}, bf16[192,1024]{1,0:T(8,128)(2,1)S(1)}, u32[]{:S(2)}, u32[]{:S(2)}) collective-permute-start(bf16[192,1024]{1,0:T(8,128)(2,1)S(1)} %get-tuple-element.23), channel_id=1, source_target_pairs={{0,2},{1,3},{2,0},{3,1},{4,6},{5,7},{6,4},{7,5},{8,10},{9,11},{10,... | collective-permute-start | bytes 1179656 | tf_op jit(solution)/shard_map/ppermute | solution.py:96
  138.6 16.7 %collective-permute-start.8 = (bf16[192,1024]{1,0:T(8,128)(2,1)S(1)}, bf16[192,1024]{1,0:T(8,128)(2,1)S(1)}, u32[]{:S(2)}, u32[]{:S(2)}) collective-permute-start(bf16[192,1024]{1,0:T(8,128)(2,1)S(1)} %get-tuple-element.21), channel_id=1, source_target_pairs={{0,3},{1,2},{2,1},{3,0},{4,7},{5,6},{6,5},{7,4},{8,11},{9,10},{10,... | collective-permute-start | bytes 1179656 | tf_op jit(solution)/shard_map/ppermute | solution.py:96
  138.9 16.5 %collective-permute-start.10 = (bf16[2,112,384]{2,1,0:T(8,128)(2,1)S(1)}, bf16[2,112,384]{2,1,0:T(8,128)(2,1)S(1)}, u32[]{:S(2)}, u32[]{:S(2)}) collective-permute-start(bf16[2,112,384]{2,1,0:T(8,128)(2,1)S(1)} %fusion.19), channel_id=1, source_target_pairs={{0,8},{4,12},{8,0},{12,4},{16,24},{20,28},{24,16},{28,20},{1,9},{5... | collective-permute-start | bytes 516104 | tf_op jit(solution)/shard_map/ppermute | solution.py:121
  155.4 2.6 %copy-start.7 = (bf16[192,4096]{1,0:T(8,128)(2,1)}, bf16[192,4096]{1,0:T(8,128)(2,1)S(1)}, u32[]{:S(2)}) copy-start(bf16[192,4096]{1,0:T(8,128)(2,1)S(1)} %constant_dynamic-update-slice_fusion) | copy-start | bytes 4718596
  155.5 14.4 %collective-permute-start.11 = (bf16[112,384]{1,0:T(8,128)(2,1)S(1)}, bf16[112,384]{1,0:T(8,128)(2,1)S(1)}, u32[]{:S(2)}, u32[]{:S(2)}) collective-permute-start(bf16[112,384]{1,0:T(8,128)(2,1)S(1)} %fusion.21), channel_id=1, source_target_pairs={{0,16},{4,20},{8,24},{12,28},{16,0},{20,4},{24,8},{28,12},{1,17},{... | collective-permute-start | bytes 258056 | tf_op jit(solution)/shard_map/ppermute | solution.py:121
  158.0 17.9 %collective-permute-start.13 = (bf16[2,112,640]{2,1,0:T(8,128)(2,1)S(1)}, bf16[2,112,640]{2,1,0:T(8,128)(2,1)S(1)}, u32[]{:S(2)}, u32[]{:S(2)}) collective-permute-start(bf16[2,112,640]{2,1,0:T(8,128)(2,1)S(1)} %fusion.17), channel_id=1, source_target_pairs={{0,16},{4,20},{8,24},{12,28},{16,0},{20,4},{24,8},{28,12},{1,17},{... | collective-permute-start | bytes 860168 | tf_op jit(solution)/shard_map/ppermute | solution.py:121
  159.4 20.6 %collective-permute-start.16 = (bf16[2,112,1024]{2,1,0:T(8,128)(2,1)S(1)}, bf16[2,112,1024]{2,1,0:T(8,128)(2,1)S(1)}, u32[]{:S(2)}, u32[]{:S(2)}) collective-permute-start(bf16[2,112,1024]{2,1,0:T(8,128)(2,1)S(1)} %fusion.14), channel_id=1, source_target_pairs={{0,8},{4,12},{8,0},{12,4},{16,24},{20,28},{24,16},{28,20},{1,9},{5... | collective-permute-start | bytes 1376264 | tf_op jit(solution)/shard_map/ppermute | solution.py:121
  176.0 5.7 %collective-permute-start.14 = (bf16[112,640]{1,0:T(8,128)(2,1)S(1)}, bf16[112,640]{1,0:T(8,128)(2,1)S(1)}, u32[]{:S(2)}, u32[]{:S(2)}) collective-permute-start(bf16[112,640]{1,0:T(8,128)(2,1)S(1)} %fusion.20), channel_id=1, source_target_pairs={{0,4},{4,0},{8,12},{12,8},{16,20},{20,16},{24,28},{28,24},{1,5},{5... | collective-permute-start | bytes 430088 | tf_op jit(solution)/shard_map/ppermute | solution.py:121
  180.0 13.2 %copy-start.1 = (bf16[896,1024]{1,0:T(8,128)(2,1)S(1)}, bf16[896,1024]{1,0:T(8,128)(2,1)}, u32[]{:S(2)}) copy-start(bf16[896,1024]{1,0:T(8,128)(2,1)} %param.14) | copy-start | bytes 5505028
  180.2 12.2 %collective-permute-start.17 = (bf16[112,1024]{1,0:T(8,128)(2,1)S(1)}, bf16[112,1024]{1,0:T(8,128)(2,1)S(1)}, u32[]{:S(2)}, u32[]{:S(2)}) collective-permute-start(bf16[112,1024]{1,0:T(8,128)(2,1)S(1)} %fusion.18), channel_id=1, source_target_pairs={{0,16},{4,20},{8,24},{12,28},{16,0},{20,4},{24,8},{28,12},{1,17},{... | collective-permute-start | bytes 688136 | tf_op jit(solution)/shard_map/ppermute | solution.py:121
Sparse Core Ops, SparseCore 0:
  51.7 38.9 all-gather.1
where the time goes:
time: 201 us; the launch traced here: 200 us
  waiting for transfers between devices  85.3 us (42%)
  local copies, waits for them, and re-layouts  28.7 us (14%)
  starting transfers between devices  25.1 us (12%)
  matrix products  21.6 us (11%)
  Pallas kernels  17.7 us (9%)
  between operations  14.5 us (7%)
  other arithmetic  6.94 us (3%)
    ppermute x9, waiting for transfers between devices, exchange(): piece = lax.ppermute(piece, axis, [(i, i ^ d) for i in range(n)])  54.7 us
    ppermute x9, waiting for transfers between devices, halving(): current = keep + lax.ppermute(away.astype(BF), axis, pairs).astype(F32)  30.6 us
    pallas_call x1, Pallas kernels, attention(): pl.pallas_call(attention_body, grid=(groups,), in_specs=[row, row, block,...  17.7 us
    ppermute x9, starting transfers between devices, halving(): current = keep + lax.ppermute(away.astype(BF), axis, pairs).astype(F32)  11.2 us
    dynamic_update_slice x9, local copies, waits for them, and re-layouts, exchange(): whole = lax.dynamic_update_slice_in_dim(whole, piece, (me ^ d) * step, join)  8.51 us
    all_to_all x1, starting transfers between devices, per_device(): lax.all_to_all(outgoing, 'dp', split_axis=0, concat_axis=0, tiled=True)  7.4 us
    ppermute x9, starting transfers between devices, exchange(): piece = lax.ppermute(piece, axis, [(i, i ^ d) for i in range(n)])  6.42 us
    dot_general x2, matrix products, weight_grad(): lax.dot_general(flat_enc, grads.reshape(-1, width), over_first, preferred...  6.12 us
  transfers between devices with their start and end apart: 20, of which 12 were waited for; matrix products, arithmetic and copies ran while one was open for 13% of the time, Pallas kernels for 0%

commit v1 on v0

--- a/solution.py
+++ b/solution.py
@@ -122,7 +122,7 @@
     return current
 
 
-def per_device(
+def staged(
     queries, cotangent, pool, enc_gain, enc_weight, k_weight, v_weight, nbr_owner, nbr_slot
 ):
     dp_count = lax.axis_size("dp")
@@ -183,6 +183,477 @@
     out = jnp.concatenate([blank, out[: seq_len - lead]], axis=0)
     merged = exchange(out, "nbr", 0, 1)
     return (merged, grad_k, grad_v)
+
+
+MESH = pl.DeviceIdType.MESH
+ROWS = 16
+PAIR = 2 * HEAD
+LAST = (((1,), (1,)), ((), ()))
+FIRST = (((0,), (0,)), ((), ()))
+
+
+def gelu(x):
+    return jax.nn.gelu(x)
+
+
+def fused_body(
+    code_ref, gain_ref, q_hbm, g_hbm, pool_hbm, encw_hbm, wk_hbm, wv_hbm,
+    att_hbm, gk_ref, gv_ref,
+    pool_v, encw_v, w_v, local, outbox, inboxes, enc, enc_t, qs, gs, os,
+    kv, dkv, dw, part_a, send_a, land_a, part_b, send_b, land_b,
+    load_sem, qg_send, qg_recv, qg_own, a2a_send, a2a_recv, gat_send, gat_recv,
+    att_send, att_recv, att_own, ra_send, ra_recv, rb_send, rb_recv,
+):
+    n_dp, n_nbr = lax.axis_size("dp"), lax.axis_size("nbr")
+    dp, nbr = lax.axis_index("dp"), lax.axis_index("nbr")
+    halves, held, _, width = local.shape
+    groups = enc.shape[1]
+    pairs, _, _ = qs.shape
+    own_rows = q_hbm.shape[0]
+    keys = groups * n_nbr * ROWS
+    per_group = n_nbr * ROWS
+    bits = n_dp.bit_length() - 1
+
+    chip, core = nbr // 2, nbr % 2
+    mate = chip * 2 + (1 - core)
+    across = ((chip + 1) * 2) % n_nbr + core
+    diagonal = ((chip + 1) * 2) % n_nbr + (1 - core)
+    nbr_peers = (across, diagonal, mate)
+    dp_peers = [(dp + k) % n_dp for k in range(1, n_dp)]
+
+    loads = [
+        pltpu.make_async_copy(pool_hbm, pool_v, load_sem.at[0]),
+        pltpu.make_async_copy(encw_hbm, encw_v, load_sem.at[1]),
+        pltpu.make_async_copy(wk_hbm, w_v.at[0], load_sem.at[2]),
+        pltpu.make_async_copy(wv_hbm, w_v.at[1], load_sem.at[3]),
+    ]
+    loads[0].start()
+    loads[1].start()
+
+    barrier = pltpu.get_barrier_semaphore()
+    for peer in nbr_peers:
+        pl.semaphore_signal(barrier, inc=1, device_id=(dp, peer), device_id_type=MESH)
+    for peer in dp_peers:
+        pl.semaphore_signal(barrier, inc=1, device_id=(peer, nbr), device_id_type=MESH)
+    pl.semaphore_wait(barrier, len(nbr_peers) + len(dp_peers))
+
+    own_at = pl.ds(pl.multiple_of(nbr * own_rows, own_rows), own_rows)
+
+    def head_cols(peer, p):
+        return pl.ds(pl.multiple_of((peer * pairs + p) * PAIR, PAIR), PAIR)
+
+    def qg_copies(p):
+        made = []
+        for t, (src, dst) in enumerate(((q_hbm, qs), (g_hbm, gs))):
+            for k, peer in enumerate(nbr_peers):
+                made.append(
+                    pltpu.make_async_remote_copy(
+                        src_ref=src.at[:, head_cols(peer, p)],
+                        dst_ref=dst.at[p, own_at, :],
+                        send_sem=qg_send.at[p, t, k],
+                        recv_sem=qg_recv.at[p, t, k],
+                        device_id=(dp, peer),
+                        device_id_type=MESH,
+                    )
+                )
+        return made
+
+    def qg_local(p):
+        return [
+            pltpu.make_async_copy(
+                src.at[:, head_cols(nbr, p)], dst.at[p, own_at, :], qg_own.at[p, t]
+            )
+            for t, (src, dst) in enumerate(((q_hbm, qs), (g_hbm, gs)))
+        ]
+
+    def start(copies):
+        for c in copies:
+            c.start()
+
+    for p in range(QG_FIRST):
+        start(qg_copies(p))
+    loads[2].start()
+    loads[3].start()
+    for p in range(pairs):
+        start(qg_local(p))
+
+    me = dp
+
+    def chosen_for(s):
+        count = jnp.int32(0)
+        picks = [jnp.int32(0)] * CAP
+        for u in range(groups):
+            code = code_ref[s * groups + u]
+            hit = code // held == me
+            for r in range(CAP):
+                picks[r] = jnp.where(hit & (count == r), code % held, picks[r])
+            count = count + jnp.where(hit, 1, 0)
+        return picks
+
+    chosen = [chosen_for(s) for s in range(n_dp)]
+    owners = [code_ref[me * groups + u] // held for u in range(groups)]
+    places = []
+    for u in range(groups):
+        rank = jnp.int32(0)
+        for w in range(u):
+            rank = rank + jnp.where(owners[w] == owners[u], 1, 0)
+        places.append(owners[u] * CAP + rank)
+
+    def a2a_copies(h):
+        return [
+            pltpu.make_async_remote_copy(
+                src_ref=outbox.at[h, peer],
+                dst_ref=inboxes[h].at[pl.ds(pl.multiple_of(me * CAP, CAP), CAP)],
+                send_sem=a2a_send.at[h, k],
+                recv_sem=a2a_recv.at[h, k],
+                device_id=(peer, nbr),
+                device_id_type=MESH,
+            )
+            for k, peer in enumerate(dp_peers)
+        ]
+
+    loads[0].wait()
+    loads[1].wait()
+    for h in range(halves):
+        x = pool_v[:, h * ROWS : (h + 1) * ROWS, :].reshape(held * ROWS, width).astype(F32)
+        mean_sq = jnp.mean(x * x, axis=-1, keepdims=True)
+        normed = (x * lax.rsqrt(mean_sq + 1e-06) * gain_ref[...]).astype(BF)
+        combined = jnp.dot(normed, encw_v[...], preferred_element_type=F32)
+        local[h] = (x + gelu(combined)).astype(BF).reshape(held, ROWS, width)
+        for s in range(n_dp):
+            for r in range(CAP):
+                outbox[h, s, r] = local[h, chosen[s][r]]
+        start(a2a_copies(h))
+        for r in range(CAP):
+            inboxes[h][me * CAP + r] = outbox[h, me, r]
+
+    tail = jnp.zeros((GROUP, PAIR), BF)
+    for p in range(pairs):
+        qs[p, groups * GROUP : (groups + 1) * GROUP, :] = tail
+        gs[p, groups * GROUP : (groups + 1) * GROUP, :] = tail
+        os[p, 0:GROUP, :] = tail
+
+    def spread(h):
+        part = enc.at[h, :, nbr]
+        return [
+            pltpu.make_async_remote_copy(
+                src_ref=part, dst_ref=part,
+                send_sem=gat_send.at[h, k], recv_sem=gat_recv.at[h, k],
+                device_id=(dp, peer), device_id_type=MESH,
+            )
+            for k, peer in enumerate((across, mate))
+        ]
+
+    def forward(h):
+        part = enc.at[h, :, across]
+        return pltpu.make_async_remote_copy(
+            src_ref=part, dst_ref=part,
+            send_sem=gat_send.at[h, 2], recv_sem=gat_recv.at[h, 2],
+            device_id=(dp, mate), device_id_type=MESH,
+        )
+
+    def transpose(h):
+        step = HEAD // per_group
+        for u in range(0, groups, step):
+            at = h * groups * per_group + u * per_group
+            block = enc[h, u : u + step].reshape(HEAD, width)
+            enc_t[:, at : at + HEAD] = block.T
+
+    for h in range(halves):
+        for c in a2a_copies(h):
+            c.wait_recv()
+        for u in range(groups):
+            enc[h, u, nbr] = inboxes[h][places[u]]
+        start(spread(h))
+        if QG_FIRST + h < pairs:
+            start(qg_copies(QG_FIRST + h))
+    for h in range(halves):
+        spread(h)[0].wait_recv()
+        forward(h).start()
+        spread(h)[1].wait_recv()
+        forward(h).wait_recv()
+        transpose(h)
+    for p in range(QG_FIRST + halves, pairs):
+        start(qg_copies(p))
+    loads[2].wait()
+    loads[3].wait()
+
+    def project(p):
+        cols = slice(p * PAIR, (p + 1) * PAIR)
+        for h in range(halves):
+            def tile(i, _):
+                u = i * TILE_GROUPS
+                rows = TILE_GROUPS * per_group
+                e = enc[h, pl.ds(u, TILE_GROUPS)].reshape(rows, width)
+                at = pl.ds(pl.multiple_of(h * groups * per_group + u * per_group, rows), rows)
+                for t in range(2):
+                    kv[t, at, :] = jnp.dot(
+                        e, w_v[t, :, cols], preferred_element_type=F32
+                    ).astype(BF)
+                return 0
+            lax.fori_loop(0, groups // TILE_GROUPS, tile, 0)
+
+    scale = HEAD ** (-0.5)
+    last_row = lax.broadcasted_iota(jnp.int32, (ROWS, PAIR), 0) == ROWS - 1
+    blank = jnp.zeros((GROUP, HEAD), BF)
+
+    def rows_of(ref, p, u):
+        here = ref[p, pl.ds(pl.multiple_of(u * GROUP + GROUP - ROWS, ROWS), ROWS), :]
+        after = ref[p, pl.ds(pl.multiple_of((u + 1) * GROUP, GROUP), GROUP), :]
+        end = jnp.where(last_row, here, after[GROUP - ROWS :])
+        got = jnp.concatenate([after[: GROUP - ROWS], end], axis=0)
+        return jnp.concatenate(
+            [
+                jnp.concatenate([got[:, :HEAD], blank], axis=1),
+                jnp.concatenate([blank, got[:, HEAD:]], axis=1),
+            ],
+            axis=0,
+        )
+
+    def key_rows(u):
+        return [
+            pl.ds(pl.multiple_of(h * groups * per_group + u * per_group, per_group), per_group)
+            for h in range(halves)
+        ]
+
+    def attend(p):
+        def several(i, _):
+            us = [i * TOGETHER + j for j in range(TOGETHER)]
+            held_now = []
+            for u in us:
+                at = key_rows(u)
+                k = jnp.concatenate([kv[0, a, :] for a in at], axis=0)
+                v = jnp.concatenate([kv[1, a, :] for a in at], axis=0)
+                q, g = rows_of(qs, p, u), rows_of(gs, p, u)
+                s = lax.dot_general(k, q, LAST, preferred_element_type=F32) * scale
+                d = lax.dot_general(v, g, LAST, preferred_element_type=F32)
+                held_now.append((v, q, g, s, d.astype(BF).astype(F32)))
+            ready = []
+            for v, q, g, s, d in held_now:
+                e = jnp.exp(s - jnp.max(s, axis=0, keepdims=True))
+                w = e * (1.0 / jnp.sum(e, axis=0, keepdims=True))
+                ds = w * (d - jnp.sum(d * w, axis=0, keepdims=True)) * scale
+                ready.append((v, q, g, w.astype(BF), ds.astype(BF)))
+            for u, (v, q, g, w, ds) in zip(us, ready):
+                o = lax.dot_general(w, v, FIRST, preferred_element_type=F32)
+                o = jnp.concatenate([o[:GROUP, :HEAD], o[GROUP:, HEAD:]], axis=1).astype(BF)
+                dk = jnp.dot(ds, q, preferred_element_type=F32).astype(BF)
+                dv = jnp.dot(w, g, preferred_element_type=F32).astype(BF)
+                for h, a in enumerate(key_rows(u)):
+                    dkv[0, a, :] = dk[h * per_group : (h + 1) * per_group]
+                    dkv[1, a, :] = dv[h * per_group : (h + 1) * per_group]
+                end = pl.ds(pl.multiple_of(u * GROUP + GROUP - ROWS, ROWS), ROWS)
+                os[p, end, :] = jnp.where(last_row, o[GROUP - ROWS :], os[p, end, :])
+                os[p, pl.ds(pl.multiple_of((u + 1) * GROUP, GROUP), GROUP), :] = o
+            return 0
+        lax.fori_loop(0, groups // TOGETHER, several, 0)
+
+    def att_copies(p):
+        return [
+            pltpu.make_async_remote_copy(
+                src_ref=os.at[p, pl.ds(pl.multiple_of(peer * own_rows, own_rows), own_rows), :],
+                dst_ref=att_hbm.at[:, head_cols(nbr, p)],
+                send_sem=att_send.at[p, k], recv_sem=att_recv.at[p, k],
+                device_id=(dp, peer), device_id_type=MESH,
+            )
+            for k, peer in enumerate(nbr_peers)
+        ]
+
+    def att_local(p):
+        return pltpu.make_async_copy(
+            os.at[p, own_at, :], att_hbm.at[:, head_cols(nbr, p)], att_own.at[p]
+        )
+
+    def weight_grads(p):
+        for t in range(2):
+            got = jnp.dot(enc_t[...], dkv[t], preferred_element_type=F32)
+            dw[p, :, :, t * PAIR : (t + 1) * PAIR] = got.reshape(n_dp, width // n_dp, PAIR)
+
+    block = width // n_dp
+    total = 2 * PAIR
+    cut = part_a.shape[-1]
+    mine = [(me // (1 << b)) % 2 for b in range(bits)]
+
+    def partner(b):
+        return me + (1 - 2 * mine[b]) * (1 << b)
+
+    pieces = (
+        (tuple(range(bits)), slice(0, cut), part_a, send_a, land_a, ra_send, ra_recv),
+        (tuple(range(1, bits)) + (0,), slice(cut, total), part_b, send_b, land_b, rb_send, rb_recv),
+    )
+
+    def count_at(k):
+        return 1 << (bits - 1 - k)
+
+    def offset_at(k):
+        return sum(count_at(j) for j in range(k))
+
+    def current(piece, p, k, a, bit):
+        order, cols, part = piece[0], piece[1], piece[2]
+        if k == 0:
+            d = bit * (1 << order[0])
+            for m in range(bits - 1):
+                d = d + ((a >> m) & 1) * (1 << order[1 + m])
+            return dw[p, d, :, cols]
+        return part[p, offset_at(k - 1) + a * 2 + bit]
+
+    def sum_copy(piece, p, k):
+        _, _, _, send, land, ssem, rsem = piece
+        at = pl.ds(offset_at(k), count_at(k))
+        return pltpu.make_async_remote_copy(
+            src_ref=send.at[p, at], dst_ref=land.at[p, at],
+            send_sem=ssem.at[p, k], recv_sem=rsem.at[p, k],
+            device_id=(partner(piece[0][k]), nbr), device_id_type=MESH,
+        )
+
+    def sum_send(p, k):
+        for piece in pieces:
+            bit = mine[piece[0][k]]
+            for a in range(count_at(k)):
+                piece[3][p, offset_at(k) + a] = current(piece, p, k, a, 1 - bit).astype(BF)
+            sum_copy(piece, p, k).start()
+
+    def sum_take(p, k):
+        for piece in pieces:
+            order, cols, part, _, land, _, _ = piece
+            bit = mine[order[k]]
+            sum_copy(piece, p, k).wait_recv()
+            for a in range(count_at(k)):
+                got = current(piece, p, k, a, bit) + land[p, offset_at(k) + a].astype(F32)
+                if k < bits - 1:
+                    part[p, offset_at(k) + a] = got
+                else:
+                    lo, hi = cols.start, cols.stop
+                    for t, out in enumerate((gk_ref, gv_ref)):
+                        a0, a1 = max(lo, t * PAIR), min(hi, (t + 1) * PAIR)
+                        if a0 < a1:
+                            base = p * PAIR - t * PAIR
+                            out[:, base + a0 : base + a1] = got[:, a0 - lo : a1 - lo]
+
+    def sum_step(p, k):
+        sum_take(p, k)
+        if k + 1 < bits:
+            sum_send(p, k + 1)
+
+    for p in range(pairs):
+        for c in qg_copies(p):
+            c.wait_recv()
+        for c in qg_local(p):
+            c.wait()
+        project(p)
+        attend(p)
+        start(att_copies(p))
+        att_local(p).start()
+        weight_grads(p)
+        sum_send(p, 0)
+        for k in range(bits):
+            if p - 1 - k >= 0:
+                sum_step(p - 1 - k, k)
+    for late in range(bits):
+        for k in range(late, bits):
+            sum_step(pairs - 1 - k + late, k)
+
+    for p in range(pairs):
+        for c in att_copies(p):
+            c.wait_recv()
+            c.wait_send()
+        att_local(p).wait()
+        for c in qg_copies(p):
+            c.wait_send()
+        for piece in pieces:
+            for k in range(bits):
+                sum_copy(piece, p, k).wait_send()
+    for h in range(halves):
+        for c in a2a_copies(h) + spread(h) + [forward(h)]:
+            c.wait_send()
+
+
+QG_FIRST = 2
+TILE_GROUPS = 4
+TOGETHER = 3
+
+
+def fused(queries, cotangent, pool, enc_gain, enc_weight, k_weight, v_weight, owner, slot):
+    n_dp, n_nbr = lax.axis_size("dp"), lax.axis_size("nbr")
+    held, tokens, width = pool.shape
+    own_rows, model = queries.shape
+    groups = owner.shape[0] // n_dp
+    halves = tokens // ROWS
+    pairs = k_weight.shape[1] // PAIR
+    bits = n_dp.bit_length() - 1
+    block = width // n_dp
+    keys = groups * n_nbr * tokens
+    steps = (1 << bits) - 1
+    cut = 3 * HEAD
+    rest = 2 * PAIR - cut
+    code = (owner * held + slot).reshape(-1)
+    anywhere = pl.BlockSpec(memory_space=pl.ANY)
+    vmem = pl.BlockSpec(memory_space=pltpu.VMEM)
+    dma = pltpu.SemaphoreType.DMA
+    out = pl.pallas_call(
+        fused_body,
+        in_specs=[pl.BlockSpec(memory_space=pltpu.SMEM), vmem] + [anywhere] * 6,
+        out_specs=[anywhere, vmem, vmem],
+        out_shape=[
+            jax.ShapeDtypeStruct(queries.shape, BF),
+            jax.ShapeDtypeStruct((block, k_weight.shape[1]), F32),
+            jax.ShapeDtypeStruct((block, v_weight.shape[1]), F32),
+        ],
+        scratch_shapes=[
+            pltpu.VMEM(pool.shape, BF),
+            pltpu.VMEM(enc_weight.shape, BF),
+            pltpu.VMEM((2,) + k_weight.shape, BF),
+            pltpu.VMEM((halves, held, ROWS, width), BF),
+            pltpu.VMEM((halves, n_dp, CAP, ROWS, width), BF),
+            [pltpu.VMEM((n_dp * CAP, ROWS, width), BF)] * halves,
+            pltpu.VMEM((halves, groups, n_nbr, ROWS, width), BF),
+            pltpu.VMEM((width, keys), BF),
+            pltpu.VMEM((pairs, (groups + 1) * GROUP, PAIR), BF),
+            pltpu.VMEM((pairs, (groups + 1) * GROUP, PAIR), BF),
+            pltpu.VMEM((pairs, (groups + 1) * GROUP, PAIR), BF),
+            pltpu.VMEM((2, keys, PAIR), BF),
+            pltpu.VMEM((2, keys, PAIR), BF),
+            pltpu.VMEM((pairs, n_dp, block, 2 * PAIR), F32),
+            pltpu.VMEM((pairs, steps, block, cut), F32),
+            pltpu.VMEM((pairs, steps, block, cut), BF),
+            pltpu.VMEM((pairs, steps, block, cut), BF),
+            pltpu.VMEM((pairs, steps, block, rest), F32),
+            pltpu.VMEM((pairs, steps, block, rest), BF),
+            pltpu.VMEM((pairs, steps, block, rest), BF),
+            dma((4,)),
+            dma((pairs, 2, 3)), dma((pairs, 2, 3)), dma((pairs, 2)),
+            dma((halves, n_dp - 1)), dma((halves, n_dp - 1)),
+            dma((halves, 3)), dma((halves, 3)),
+            dma((pairs, 3)), dma((pairs, 3)), dma((pairs,)),
+            dma((pairs, bits)), dma((pairs, bits)), dma((pairs, bits)), dma((pairs, bits)),
+        ],
+        compiler_params=pltpu.CompilerParams(
+            collective_id=0, has_side_effects=True, vmem_limit_bytes=58 * 2**20
+        ),
+    )(code, enc_gain.reshape(1, -1), queries, cotangent, pool, enc_weight, k_weight, v_weight)
+    return tuple(out)
+
+
+def per_device(
+    queries, cotangent, pool, enc_gain, enc_weight, k_weight, v_weight, nbr_owner, nbr_slot
+):
+    n_dp, n_nbr = lax.axis_size("dp"), lax.axis_size("nbr")
+    _, tokens, width = pool.shape
+    groups = nbr_owner.shape[0] // n_dp
+    args = (
+        queries, cotangent, pool, enc_gain, enc_weight, k_weight, v_weight, nbr_owner, nbr_slot
+    )
+    fits = (
+        n_nbr == 4
+        and n_dp & (n_dp - 1) == 0
+        and width % (n_dp * ROWS) == 0
+        and tokens % ROWS == 0
+        and k_weight.shape[1] % PAIR == 0
+        and groups % TILE_GROUPS == 0
+        and groups % TOGETHER == 0
+        and HEAD % (n_nbr * ROWS) == 0
+    )
+    return fused(*args) if fits else staged(*args)
 
 
 def solution(mesh):

time: 201 us -> 117 us (0.58)
  Pallas kernels: 17.7 us -> 110 us
  waiting for transfers between devices: 85.3 us -> 0 us
  starting transfers between devices: 25.1 us -> 0 us
  local copies, waits for them, and re-layouts: 28.7 us -> 5.59 us
  matrix products: 21.6 us -> 0 us
  between operations: 14.5 us -> 0.66 us
  other arithmetic: 6.94 us -> 1.19 us
    pallas_call x1, Pallas kernels: 17.7 us -> 110 us  [fused(): pl.pallas_call(fused_body, in_specs=[pl.BlockSpec(memory_space=pltpu.SMEM...]
    ppermute x18 -> x0, waiting for transfers between devices: 85.3 us -> none  [the longest x9 54.7 us: exchange(): piece = lax.ppermute(piece, axis, [(i, i ^ d) for i in range(n)])]
    dot_general x7 -> x0, matrix products: 21.6 us -> none  [the longest x2 6.12 us: weight_grad(): lax.dot_general(flat_enc, grads.reshape(-1, width), over_first, preferred...]
    ppermute x18 -> x0, starting transfers between devices: 17.6 us -> none  [the longest x9 11.2 us: halving(): current = keep + lax.ppermute(away.astype(BF), axis, pairs).astype(F32)]
    dynamic_update_slice x9 -> x0, local copies, waits for them, and re-layouts: 8.51 us -> none  [exchange(): whole = lax.dynamic_update_slice_in_dim(whole, piece, (me ^ d) * step, join)]
    all_to_all x1 -> x0, starting transfers between devices: 7.4 us -> none  [per_device(): lax.all_to_all(outgoing, 'dp', split_axis=0, concat_axis=0, tiled=True)]
    dynamic_slice x3 -> x0, local copies, waits for them, and re-layouts: 4.76 us -> none  [exchange(): piece = lax.dynamic_slice_in_dim(x, (me ^ d) * span, span, split)]
    dot_general x1 -> x0, local copies, waits for them, and re-layouts: 4.64 us -> none  [weight_grad(): lax.dot_general(flat_enc, grads.reshape(-1, width), over_first, preferred...]
  transfers between devices with their start and end apart: 20 -> 0, of which waited for: 12 -> 0; matrix products, arithmetic and copies ran while one was open for 13% -> 0% of each run, Pallas kernels for 0% -> 0%
where the time goes in v1:
time: 117 us
  Pallas kernels  110 us (94%)
  local copies, waits for them, and re-layouts  5.59 us (5%)
  other arithmetic  1.19 us (1%)
    pallas_call x1, Pallas kernels, fused(): pl.pallas_call(fused_body, in_specs=[pl.BlockSpec(memory_space=pltpu.SMEM...  110 us
    unnamed x7, local copies, waits for them, and re-layouts  4.32 us

profile of v1, /device:TPU:0, one launch (start us, length us, event | category | flops | bytes accessed | tf_op | source)
XLA Modules:
  0.0 117.2 jit_solution(17471881150931165955)
XLA Ops:
  0.6 1.2 %add_bitcast_fusion.code_ref = s32[96]{0:T(128)} fusion(s32[96,1]{0,1:T(1,128)} %param.17, s32[96,1]{0,1:T(1,128)} %param.16), kind=kLoop, calls=%fused_computation | loop fusion | flops 192 | bytes 1152 | tf_op jit(solution)/shard_map/reshape | solution.py:589
  1.8 1.3 %reshape.13.gain_ref = f32[1,896]{1,0:T(1,128)} reshape(f32[896]{0:T(1024)} %param.12) | data formatting | bytes 7168 | tf_op jit(solution)/shard_map/reshape | solution.py:633
  3.1 109.8 %shard_map.112 = (bf16[192,4096]{1,0:T(8,128)(2,1)}, f32[112,1024]{1,0:T(8,128)}, f32[112,1024]{1,0:T(8,128)}) custom-call(s32[96]{0:T(128)} %add_bitcast_fusion.code_ref, f32[1,896]{1,0:T(1,128)} %reshape.13.gain_ref, bf16[192,4096]{1,0:T(8,128)(2,1)} %q_hbm.1, bf16[192,4096]{1,0:T(8,128)(2,1)} %g_hbm.1, bf16[8,32,896]{2,1,0:T(8,128)(2,1)} %pool_hbm.1, ...), custom_call_target="tpu_custom_call" | custom-call | tf_op jit(solution)/shard_map/pallas_call | solution.py:593
  112.9 0.0 copy-start.1
  112.9 0.0 copy-start
  112.9 2.8 %copy.15 = bf16[192,4096]{1,0:T(8,128)(2,1)} copy(bf16[192,4096]{1,0:T(8,128)(2,1)} %get-tuple-element.6) | data formatting | bytes 3145728
  115.7 0.0 copy-done.1
  115.7 0.8 copy.16
  116.5 0.0 copy-done
  116.5 0.8 copy.17
Async XLA Ops:
  112.9 2.8 %copy-start.1 = (f32[112,1024]{1,0:T(8,128)S(1)}, f32[112,1024]{1,0:T(8,128)}, u32[]{:S(2)}) copy-start(f32[112,1024]{1,0:T(8,128)} %get-tuple-element.7) | copy-start | bytes 1376260
  112.9 3.6 %copy-start = (f32[112,1024]{1,0:T(8,128)S(1)}, f32[112,1024]{1,0:T(8,128)}, u32[]{:S(2)}) copy-start(f32[112,1024]{1,0:T(8,128)} %get-tuple-element.8) | copy-start | bytes 1376260

commit v2 on v1

--- a/solution.py
+++ b/solution.py
@@ -317,7 +317,7 @@
     for h in range(halves):
         x = pool_v[:, h * ROWS : (h + 1) * ROWS, :].reshape(held * ROWS, width).astype(F32)
         mean_sq = jnp.mean(x * x, axis=-1, keepdims=True)
-        normed = (x * lax.rsqrt(mean_sq + 1e-06) * gain_ref[...]).astype(BF)
+        normed = (x * lax.rsqrt(mean_sq + 1e-06) * gain_ref[...].reshape(1, width)).astype(BF)
         combined = jnp.dot(normed, encw_v[...], preferred_element_type=F32)
         local[h] = (x + gelu(combined)).astype(BF).reshape(held, ROWS, width)
         for s in range(n_dp):
@@ -365,15 +365,13 @@
         for u in range(groups):
             enc[h, u, nbr] = inboxes[h][places[u]]
         start(spread(h))
-        if QG_FIRST + h < pairs:
-            start(qg_copies(QG_FIRST + h))
     for h in range(halves):
         spread(h)[0].wait_recv()
         forward(h).start()
         spread(h)[1].wait_recv()
         forward(h).wait_recv()
         transpose(h)
-    for p in range(QG_FIRST + halves, pairs):
+    for p in range(QG_FIRST, pairs):
         start(qg_copies(p))
     loads[2].wait()
     loads[3].wait()
@@ -568,7 +566,7 @@
             c.wait_send()
 
 
-QG_FIRST = 2
+QG_FIRST = 1
 TILE_GROUPS = 4
 TOGETHER = 3
 
@@ -630,7 +628,7 @@
         compiler_params=pltpu.CompilerParams(
             collective_id=0, has_side_effects=True, vmem_limit_bytes=58 * 2**20
         ),
-    )(code, enc_gain.reshape(1, -1), queries, cotangent, pool, enc_weight, k_weight, v_weight)
+    )(code, enc_gain, queries, cotangent, pool, enc_weight, k_weight, v_weight)
     return tuple(out)
 
 

time: 117 us -> 103 us (0.88)
  Pallas kernels: 110 us -> 97.1 us
  local copies, waits for them, and re-layouts: 5.59 us -> 4.32 us
    pallas_call x1, Pallas kernels: 110 us -> 97.1 us  [fused(): pl.pallas_call(fused_body, in_specs=[pl.BlockSpec(memory_space=pltpu.SMEM...]
    reshape x1 -> x0, local copies, waits for them, and re-layouts: 1.27 us -> none  [fused(): enc_gain.reshape(1, -1)]
where the time goes in v2:
time: 103 us
  Pallas kernels  97.1 us (94%)
  local copies, waits for them, and re-layouts  4.32 us (4%)
  other arithmetic  1.19 us (1%)
    pallas_call x1, Pallas kernels, fused(): pl.pallas_call(fused_body, in_specs=[pl.BlockSpec(memory_space=pltpu.SMEM...  97.1 us
    unnamed x7, local copies, waits for them, and re-layouts  4.32 us

profile of v2, /device:TPU:0, one launch (start us, length us, event | category | flops | bytes accessed | tf_op | source)
XLA Modules:
  0.0 103.3 jit_solution(16043545629268317202)
XLA Ops:
  0.6 1.2 %add_bitcast_fusion.code_ref = s32[96]{0:T(128)} fusion(s32[96,1]{0,1:T(1,128)} %param.17, s32[96,1]{0,1:T(1,128)} %param.16), kind=kLoop, calls=%fused_computation | loop fusion | flops 192 | bytes 1152 | tf_op jit(solution)/shard_map/reshape | solution.py:587
  1.8 97.1 %shard_map.112 = (bf16[192,4096]{1,0:T(8,128)(2,1)}, f32[112,1024]{1,0:T(8,128)}, f32[112,1024]{1,0:T(8,128)}) custom-call(s32[96]{0:T(128)} %add_bitcast_fusion.code_ref, f32[896]{0:T(1024)} %gain_ref.1, bf16[192,4096]{1,0:T(8,128)(2,1)} %q_hbm.1, bf16[192,4096]{1,0:T(8,128)(2,1)} %g_hbm.1, bf16[8,32,896]{2,1,0:T(8,128)(2,1)} %pool_hbm.1, ...), custom_call_target="tpu_custom_call" | custom-call | tf_op jit(solution)/shard_map/pallas_call | solution.py:591
  98.9 0.0 copy-start.1
  98.9 0.0 copy-start
  98.9 2.8 %copy.15 = bf16[192,4096]{1,0:T(8,128)(2,1)} copy(bf16[192,4096]{1,0:T(8,128)(2,1)} %get-tuple-element.6) | data formatting | bytes 3145728
  101.7 0.0 copy-done.1
  101.7 0.8 copy.16
  102.5 0.0 copy-done
  102.5 0.8 copy.17
Async XLA Ops:
  98.9 2.8 %copy-start.1 = (f32[112,1024]{1,0:T(8,128)S(1)}, f32[112,1024]{1,0:T(8,128)}, u32[]{:S(2)}) copy-start(f32[112,1024]{1,0:T(8,128)} %get-tuple-element.7) | copy-start | bytes 1376260
  98.9 3.6 %copy-start = (f32[112,1024]{1,0:T(8,128)S(1)}, f32[112,1024]{1,0:T(8,128)}, u32[]{:S(2)}) copy-start(f32[112,1024]{1,0:T(8,128)} %get-tuple-element.8) | copy-start | bytes 1376260

commit v3 on v2

--- a/solution.py
+++ b/solution.py
@@ -199,15 +199,16 @@
 def fused_body(
     code_ref, gain_ref, q_hbm, g_hbm, pool_hbm, encw_hbm, wk_hbm, wv_hbm,
     att_hbm, gk_ref, gv_ref,
-    pool_v, encw_v, w_v, local, outbox, inboxes, enc, enc_t, qs, gs, os,
-    kv, dkv, dw, part_a, send_a, land_a, part_b, send_b, land_b,
+    pool_v, encw_v, w_v, local, outboxes, inboxes, enc, enc_t, qs, gs, os,
+    kv, dkv, dw, parts_a, sends_a, lands_a, parts_b, sends_b, lands_b,
     load_sem, qg_send, qg_recv, qg_own, a2a_send, a2a_recv, gat_send, gat_recv,
     att_send, att_recv, att_own, ra_send, ra_recv, rb_send, rb_recv,
 ):
     n_dp, n_nbr = lax.axis_size("dp"), lax.axis_size("nbr")
     dp, nbr = lax.axis_index("dp"), lax.axis_index("nbr")
-    halves, held, _, width = local.shape
-    groups = enc.shape[1]
+    held, tokens, width = pool_v.shape
+    halves, groups = enc.shape[:2]
+    cuts = column_cuts(halves, width)
     pairs, _, _ = qs.shape
     own_rows = q_hbm.shape[0]
     keys = groups * n_nbr * ROWS
@@ -235,8 +236,6 @@
         pl.semaphore_signal(barrier, inc=1, device_id=(dp, peer), device_id_type=MESH)
     for peer in dp_peers:
         pl.semaphore_signal(barrier, inc=1, device_id=(peer, nbr), device_id_type=MESH)
-    pl.semaphore_wait(barrier, len(nbr_peers) + len(dp_peers))
-
     own_at = pl.ds(pl.multiple_of(nbr * own_rows, own_rows), own_rows)
 
     def head_cols(peer, p):
@@ -270,13 +269,6 @@
         for c in copies:
             c.start()
 
-    for p in range(QG_FIRST):
-        start(qg_copies(p))
-    loads[2].start()
-    loads[3].start()
-    for p in range(pairs):
-        start(qg_local(p))
-
     me = dp
 
     def chosen_for(s):
@@ -299,33 +291,50 @@
             rank = rank + jnp.where(owners[w] == owners[u], 1, 0)
         places.append(owners[u] * CAP + rank)
 
-    def a2a_copies(h):
+    def a2a_copies(n):
         return [
             pltpu.make_async_remote_copy(
-                src_ref=outbox.at[h, peer],
-                dst_ref=inboxes[h].at[pl.ds(pl.multiple_of(me * CAP, CAP), CAP)],
-                send_sem=a2a_send.at[h, k],
-                recv_sem=a2a_recv.at[h, k],
+                src_ref=outboxes[n].at[peer],
+                dst_ref=inboxes[n].at[pl.ds(pl.multiple_of(me * CAP, CAP), CAP)],
+                send_sem=a2a_send.at[n, k],
+                recv_sem=a2a_recv.at[n, k],
                 device_id=(peer, nbr),
                 device_id_type=MESH,
             )
             for k, peer in enumerate(dp_peers)
         ]
 
+    def encoded(x):
+        x = x.astype(F32)
+        mean_sq = jnp.mean(x * x, axis=-1, keepdims=True)
+        normed = (x * lax.rsqrt(mean_sq + 1e-06) * gain_ref[...].reshape(1, width)).astype(BF)
+        combined = jnp.dot(normed, encw_v[...], preferred_element_type=F32)
+        return (x + jax.nn.gelu(combined)).astype(BF)
+
+    def fill_outbox(n, block_at):
+        for s in range(n_dp):
+            for r in range(CAP):
+                outboxes[n][s, r] = block_at(chosen[s][r])
+
+    def keep_own(n):
+        for r in range(CAP):
+            inboxes[n][me * CAP + r] = outboxes[n][me, r]
+
     loads[0].wait()
     loads[1].wait()
     for h in range(halves):
-        x = pool_v[:, h * ROWS : (h + 1) * ROWS, :].reshape(held * ROWS, width).astype(F32)
-        mean_sq = jnp.mean(x * x, axis=-1, keepdims=True)
-        normed = (x * lax.rsqrt(mean_sq + 1e-06) * gain_ref[...].reshape(1, width)).astype(BF)
-        combined = jnp.dot(normed, encw_v[...], preferred_element_type=F32)
-        local[h] = (x + gelu(combined)).astype(BF).reshape(held, ROWS, width)
-        for s in range(n_dp):
-            for r in range(CAP):
-                outbox[h, s, r] = local[h, chosen[s][r]]
-        start(a2a_copies(h))
-        for r in range(CAP):
-            inboxes[h][me * CAP + r] = outbox[h, me, r]
+        x = pool_v[:, h * ROWS : (h + 1) * ROWS, :].reshape(held * ROWS, width)
+        local[h] = encoded(x).reshape(held, ROWS, width)
+    for n, (h, cols) in enumerate(cuts):
+        fill_outbox(n, lambda b: local[h, b, :, cols])
+        keep_own(n)
+    pl.semaphore_wait(barrier, len(nbr_peers) + len(dp_peers))
+    start(a2a_copies(0))
+    start(qg_copies(0))
+    loads[2].start()
+    loads[3].start()
+    for p in range(pairs):
+        start(qg_local(p))
 
     tail = jnp.zeros((GROUP, PAIR), BF)
     for p in range(pairs):
@@ -333,22 +342,24 @@
         gs[p, groups * GROUP : (groups + 1) * GROUP, :] = tail
         os[p, 0:GROUP, :] = tail
 
-    def spread(h):
-        part = enc.at[h, :, nbr]
+    def spread(n):
+        h, cols = cuts[n]
+        part = enc.at[h, :, nbr, :, cols]
         return [
             pltpu.make_async_remote_copy(
                 src_ref=part, dst_ref=part,
-                send_sem=gat_send.at[h, k], recv_sem=gat_recv.at[h, k],
+                send_sem=gat_send.at[n, k], recv_sem=gat_recv.at[n, k],
                 device_id=(dp, peer), device_id_type=MESH,
             )
             for k, peer in enumerate((across, mate))
         ]
 
-    def forward(h):
-        part = enc.at[h, :, across]
+    def forward(n):
+        h, cols = cuts[n]
+        part = enc.at[h, :, across, :, cols]
         return pltpu.make_async_remote_copy(
             src_ref=part, dst_ref=part,
-            send_sem=gat_send.at[h, 2], recv_sem=gat_recv.at[h, 2],
+            send_sem=gat_send.at[n, 2], recv_sem=gat_recv.at[n, 2],
             device_id=(dp, mate), device_id_type=MESH,
         )
 
@@ -359,26 +370,24 @@
             block = enc[h, u : u + step].reshape(HEAD, width)
             enc_t[:, at : at + HEAD] = block.T
 
-    for h in range(halves):
-        for c in a2a_copies(h):
+    if EARLY:
+        for c in qg_copies(0):
+            c.wait_recv()
+        start(qg_copies(1)[:EARLY])
+    for n, (h, cols) in enumerate(cuts):
+        if n + 1 < len(cuts):
+            for c in a2a_copies(n):
+                c.wait_send()
+            start(a2a_copies(n + 1))
+        for c in a2a_copies(n):
             c.wait_recv()
         for u in range(groups):
-            enc[h, u, nbr] = inboxes[h][places[u]]
-        start(spread(h))
-    for h in range(halves):
-        spread(h)[0].wait_recv()
-        forward(h).start()
-        spread(h)[1].wait_recv()
-        forward(h).wait_recv()
-        transpose(h)
-    for p in range(QG_FIRST, pairs):
-        start(qg_copies(p))
-    loads[2].wait()
-    loads[3].wait()
-
-    def project(p):
+            enc[h, u, nbr, :, cols] = inboxes[n][places[u]]
+        start(spread(n))
+
+    def project(p, hs):
         cols = slice(p * PAIR, (p + 1) * PAIR)
-        for h in range(halves):
+        for h in hs:
             def tile(i, _):
                 u = i * TILE_GROUPS
                 rows = TILE_GROUPS * per_group
@@ -467,18 +476,21 @@
             got = jnp.dot(enc_t[...], dkv[t], preferred_element_type=F32)
             dw[p, :, :, t * PAIR : (t + 1) * PAIR] = got.reshape(n_dp, width // n_dp, PAIR)
 
-    block = width // n_dp
-    total = 2 * PAIR
-    cut = part_a.shape[-1]
     mine = [(me // (1 << b)) % 2 for b in range(bits)]
 
     def partner(b):
         return me + (1 - 2 * mine[b]) * (1 << b)
 
-    pieces = (
-        (tuple(range(bits)), slice(0, cut), part_a, send_a, land_a, ra_send, ra_recv),
-        (tuple(range(1, bits)) + (0,), slice(cut, total), part_b, send_b, land_b, rb_send, rb_recv),
-    )
+    def pieces_of(p):
+        made = []
+        orders = (tuple(range(bits)), tuple(range(1, bits)) + (0,))
+        stacks = ((parts_a, sends_a, lands_a), (parts_b, sends_b, lands_b))
+        for n, (lo, hi) in enumerate(((0, CUTS[p]), (CUTS[p], 2 * PAIR))):
+            if lo < hi:
+                part, send, land = (x[p] for x in stacks[n])
+                sems = (ra_send, ra_recv) if n == 0 else (rb_send, rb_recv)
+                made.append((orders[n], slice(lo, hi), part, send, land) + sems)
+        return made
 
     def count_at(k):
         return 1 << (bits - 1 - k)
@@ -493,33 +505,33 @@
             for m in range(bits - 1):
                 d = d + ((a >> m) & 1) * (1 << order[1 + m])
             return dw[p, d, :, cols]
-        return part[p, offset_at(k - 1) + a * 2 + bit]
+        return part[offset_at(k - 1) + a * 2 + bit]
 
     def sum_copy(piece, p, k):
         _, _, _, send, land, ssem, rsem = piece
         at = pl.ds(offset_at(k), count_at(k))
         return pltpu.make_async_remote_copy(
-            src_ref=send.at[p, at], dst_ref=land.at[p, at],
+            src_ref=send.at[at], dst_ref=land.at[at],
             send_sem=ssem.at[p, k], recv_sem=rsem.at[p, k],
             device_id=(partner(piece[0][k]), nbr), device_id_type=MESH,
         )
 
     def sum_send(p, k):
-        for piece in pieces:
+        for piece in pieces_of(p):
             bit = mine[piece[0][k]]
             for a in range(count_at(k)):
-                piece[3][p, offset_at(k) + a] = current(piece, p, k, a, 1 - bit).astype(BF)
+                piece[3][offset_at(k) + a] = current(piece, p, k, a, 1 - bit).astype(BF)
             sum_copy(piece, p, k).start()
 
     def sum_take(p, k):
-        for piece in pieces:
+        for piece in pieces_of(p):
             order, cols, part, _, land, _, _ = piece
             bit = mine[order[k]]
             sum_copy(piece, p, k).wait_recv()
             for a in range(count_at(k)):
-                got = current(piece, p, k, a, bit) + land[p, offset_at(k) + a].astype(F32)
+                got = current(piece, p, k, a, bit) + land[offset_at(k) + a].astype(F32)
                 if k < bits - 1:
-                    part[p, offset_at(k) + a] = got
+                    part[offset_at(k) + a] = got
                 else:
                     lo, hi = cols.start, cols.stop
                     for t, out in enumerate((gk_ref, gv_ref)):
@@ -533,23 +545,56 @@
         if k + 1 < bits:
             sum_send(p, k + 1)
 
+    def collect(n):
+        spread(n)[0].wait_recv()
+        forward(n).start()
+
+    def settle(n):
+        spread(n)[1].wait_recv()
+        forward(n).wait_recv()
+
+    for h in range(halves):
+        ns = [n for n in range(len(cuts)) if cuts[n][0] == h]
+        for n in ns:
+            collect(n)
+        if h == 0:
+            loads[2].wait()
+            loads[3].wait()
+        if h == halves - 1:
+            start(qg_copies(1)[EARLY:])
+            start(qg_copies(2)[:SECOND])
+        for n in ns:
+            settle(n)
+        project(0, [h])
+        transpose(h)
     for p in range(pairs):
-        for c in qg_copies(p):
-            c.wait_recv()
+        if p == 0:
+            start(qg_copies(2)[SECOND:])
+        if 0 < p < pairs - 2:
+            start(qg_copies(p + 2))
+        if p:
+            project(p, range(halves))
+        if p == 0 and not EARLY or p > 0:
+            for c in qg_copies(p):
+                c.wait_recv()
         for c in qg_local(p):
             c.wait()
-        project(p)
+        if p == HOLD:
+            for before in range(p):
+                start(att_copies(before))
         attend(p)
-        start(att_copies(p))
+        if p >= HOLD:
+            start(att_copies(p))
         att_local(p).start()
         weight_grads(p)
         sum_send(p, 0)
         for k in range(bits):
             if p - 1 - k >= 0:
                 sum_step(p - 1 - k, k)
-    for late in range(bits):
-        for k in range(late, bits):
-            sum_step(pairs - 1 - k + late, k)
+    for k in range(bits):
+        for back in range(1, bits - k):
+            sum_step(pairs - 1 - back, k + back)
+        sum_step(pairs - 1, k)
 
     for p in range(pairs):
         for c in att_copies(p):
@@ -558,15 +603,30 @@
         att_local(p).wait()
         for c in qg_copies(p):
             c.wait_send()
-        for piece in pieces:
+        for piece in pieces_of(p):
             for k in range(bits):
                 sum_copy(piece, p, k).wait_send()
-    for h in range(halves):
-        for c in a2a_copies(h) + spread(h) + [forward(h)]:
+    for n in range(len(cuts)):
+        for c in spread(n) + [forward(n)]:
             c.wait_send()
-
-
-QG_FIRST = 1
+    for c in a2a_copies(len(cuts) - 1):
+        c.wait_send()
+
+
+EARLY = 3
+SECOND = 0
+HOLD = 3
+CUTS = (256, 384, 384, 384)
+
+
+def column_cuts(halves, width):
+    middle = (width // HEAD + 1) // 2 * HEAD
+    cuts = [(0, slice(0, width))]
+    for h in range(1, halves):
+        cuts += [(h, slice(0, middle)), (h, slice(middle, width))]
+    return cuts
+
+
 TILE_GROUPS = 4
 TOGETHER = 3
 
@@ -582,8 +642,9 @@
     block = width // n_dp
     keys = groups * n_nbr * tokens
     steps = (1 << bits) - 1
-    cut = 3 * HEAD
-    rest = 2 * PAIR - cut
+    cuts = column_cuts(halves, width)
+    wide = [cols.stop - cols.start for _, cols in cuts]
+    rest = [max(2 * PAIR - cut, HEAD) for cut in CUTS]
     code = (owner * held + slot).reshape(-1)
     anywhere = pl.BlockSpec(memory_space=pl.ANY)
     vmem = pl.BlockSpec(memory_space=pltpu.VMEM)
@@ -591,9 +652,9 @@
     out = pl.pallas_call(
         fused_body,
         in_specs=[pl.BlockSpec(memory_space=pltpu.SMEM), vmem] + [anywhere] * 6,
-        out_specs=[anywhere, vmem, vmem],
+        out_specs=[vmem, vmem, vmem],
         out_shape=[
-            jax.ShapeDtypeStruct(queries.shape, BF),
+            pltpu.VMEM(queries.shape, BF),
             jax.ShapeDtypeStruct((block, k_weight.shape[1]), F32),
             jax.ShapeDtypeStruct((block, v_weight.shape[1]), F32),
         ],
@@ -602,8 +663,8 @@
             pltpu.VMEM(enc_weight.shape, BF),
             pltpu.VMEM((2,) + k_weight.shape, BF),
             pltpu.VMEM((halves, held, ROWS, width), BF),
-            pltpu.VMEM((halves, n_dp, CAP, ROWS, width), BF),
-            [pltpu.VMEM((n_dp * CAP, ROWS, width), BF)] * halves,
+            [pltpu.VMEM((n_dp, CAP, ROWS, w), BF) for w in wide],
+            [pltpu.VMEM((n_dp * CAP, ROWS, w), BF) for w in wide],
             pltpu.VMEM((halves, groups, n_nbr, ROWS, width), BF),
             pltpu.VMEM((width, keys), BF),
             pltpu.VMEM((pairs, (groups + 1) * GROUP, PAIR), BF),
@@ -612,16 +673,16 @@
             pltpu.VMEM((2, keys, PAIR), BF),
             pltpu.VMEM((2, keys, PAIR), BF),
             pltpu.VMEM((pairs, n_dp, block, 2 * PAIR), F32),
-            pltpu.VMEM((pairs, steps, block, cut), F32),
-            pltpu.VMEM((pairs, steps, block, cut), BF),
-            pltpu.VMEM((pairs, steps, block, cut), BF),
-            pltpu.VMEM((pairs, steps, block, rest), F32),
-            pltpu.VMEM((pairs, steps, block, rest), BF),
-            pltpu.VMEM((pairs, steps, block, rest), BF),
+            [pltpu.VMEM((steps, block, n), F32) for n in CUTS],
+            [pltpu.VMEM((steps, block, n), BF) for n in CUTS],
+            [pltpu.VMEM((steps, block, n), BF) for n in CUTS],
+            [pltpu.VMEM((steps, block, n), F32) for n in rest],
+            [pltpu.VMEM((steps, block, n), BF) for n in rest],
+            [pltpu.VMEM((steps, block, n), BF) for n in rest],
             dma((4,)),
             dma((pairs, 2, 3)), dma((pairs, 2, 3)), dma((pairs, 2)),
-            dma((halves, n_dp - 1)), dma((halves, n_dp - 1)),
-            dma((halves, 3)), dma((halves, 3)),
+            dma((len(cuts), n_dp - 1)), dma((len(cuts), n_dp - 1)),
+            dma((len(cuts), 3)), dma((len(cuts), 3)),
             dma((pairs, 3)), dma((pairs, 3)), dma((pairs,)),
             dma((pairs, bits)), dma((pairs, bits)), dma((pairs, bits)), dma((pairs, bits)),
         ],
@@ -646,7 +707,8 @@
         and n_dp & (n_dp - 1) == 0
         and width % (n_dp * ROWS) == 0
         and tokens % ROWS == 0
-        and k_weight.shape[1] % PAIR == 0
+        and tokens > ROWS
+        and k_weight.shape[1] == PAIR * len(CUTS)
         and groups % TILE_GROUPS == 0
         and groups % TOGETHER == 0
         and HEAD % (n_nbr * ROWS) == 0

time: 103 us -> 100 us (0.971)
  Pallas kernels: 97.1 us -> 95.5 us
  local copies, waits for them, and re-layouts: 4.32 us -> 2.78 us
    pallas_call x1, Pallas kernels: 97.1 us -> 95.5 us  [fused(): pl.pallas_call(fused_body, in_specs=[pl.BlockSpec(memory_space=pltpu.SMEM...]
    unnamed x7, local copies, waits for them, and re-layouts: 4.32 us -> 2.78 us
where the time goes in v3:
time: 100 us
  Pallas kernels  95.5 us (96%)
  local copies, waits for them, and re-layouts  2.78 us (3%)
  other arithmetic  1.19 us (1%)
    pallas_call x1, Pallas kernels, fused(): pl.pallas_call(fused_body, in_specs=[pl.BlockSpec(memory_space=pltpu.SMEM...  95.5 us
    unnamed x7, local copies, waits for them, and re-layouts  2.78 us

profile of v3, /device:TPU:0, one launch (start us, length us, event | category | flops | bytes accessed | tf_op | source)
XLA Modules:
  0.0 100.1 jit_solution(1798761233390270113)
XLA Ops:
  0.6 1.2 %add_bitcast_fusion.code_ref = s32[96]{0:T(128)} fusion(s32[96,1]{0,1:T(1,128)} %param.17, s32[96,1]{0,1:T(1,128)} %param.16), kind=kLoop, calls=%fused_computation | loop fusion | flops 192 | bytes 1152 | tf_op jit(solution)/shard_map/reshape | solution.py:648
  1.8 95.5 %shard_map.112 = (bf16[192,4096]{1,0:T(8,128)(2,1)S(1)}, f32[112,1024]{1,0:T(8,128)}, f32[112,1024]{1,0:T(8,128)}) custom-call(s32[96]{0:T(128)} %add_bitcast_fusion.code_ref, f32[896]{0:T(1024)} %gain_ref.1, bf16[192,4096]{1,0:T(8,128)(2,1)} %q_hbm.1, bf16[192,4096]{1,0:T(8,128)(2,1)} %g_hbm.1, bf16[8,32,896]{2,1,0:T(8,128)(2,1)} %pool_hbm.1, ...), custom_call_target="tpu_custom_call" | custom-call | tf_op jit(solution)/shard_map/pallas_call | solution.py:652
  97.3 0.0 copy-start.1
  97.3 0.0 copy-start
  97.3 1.1 %copy.15 = bf16[192,4096]{1,0:T(8,128)(2,1)} copy(bf16[192,4096]{1,0:T(8,128)(2,1)S(1)} %get-tuple-element.3) | data formatting | bytes 3145728
  98.5 0.1 copy-done.1
  98.6 0.8 copy.16
  99.3 0.0 copy-done
  99.3 0.8 copy.17
Async XLA Ops:
  97.3 1.3 %copy-start.1 = (f32[112,1024]{1,0:T(8,128)S(1)}, f32[112,1024]{1,0:T(8,128)}, u32[]{:S(2)}) copy-start(f32[112,1024]{1,0:T(8,128)} %get-tuple-element.10) | copy-start | bytes 1376260
  97.3 2.0 %copy-start = (f32[112,1024]{1,0:T(8,128)S(1)}, f32[112,1024]{1,0:T(8,128)}, u32[]{:S(2)}) copy-start(f32[112,1024]{1,0:T(8,128)} %get-tuple-element.11) | copy-start | bytes 1376260

commit v4 on v3

--- a/solution.py
+++ b/solution.py
@@ -655,8 +655,8 @@
         out_specs=[vmem, vmem, vmem],
         out_shape=[
             pltpu.VMEM(queries.shape, BF),
-            jax.ShapeDtypeStruct((block, k_weight.shape[1]), F32),
-            jax.ShapeDtypeStruct((block, v_weight.shape[1]), F32),
+            pltpu.VMEM((block, k_weight.shape[1]), F32),
+            pltpu.VMEM((block, v_weight.shape[1]), F32),
         ],
         scratch_shapes=[
             pltpu.VMEM(pool.shape, BF),

time: 100 us -> 99.2 us (level)
  Pallas kernels: 95.5 us -> 94.5 us
    unnamed x7 -> x3, local copies, waits for them, and re-layouts: 2.78 us -> 2.68 us
where the time goes in v4:
time: 99.2 us; the launch traced here: 99 us
  Pallas kernels  94.5 us (95%)
  local copies, waits for them, and re-layouts  2.68 us (3%)
  other arithmetic  1.19 us (1%)
    pallas_call x1, Pallas kernels, fused(): pl.pallas_call(fused_body, in_specs=[pl.BlockSpec(memory_space=pltpu.SMEM...  94.5 us
    unnamed x3, local copies, waits for them, and re-layouts  2.68 us

profile of v4, /device:TPU:0, one launch (start us, length us, event | category | flops | bytes accessed | tf_op | source)
XLA Modules:
  0.0 99.0 jit_solution(9279833213709326607)
XLA Ops:
  0.6 1.2 %add_bitcast_fusion.code_ref = s32[96]{0:T(128)} fusion(s32[96,1]{0,1:T(1,128)} %param.17, s32[96,1]{0,1:T(1,128)} %param.16), kind=kLoop, calls=%fused_computation | loop fusion | flops 192 | bytes 1152 | tf_op jit(solution)/shard_map/reshape | solution.py:648
  1.8 94.5 %shard_map.112 = (bf16[192,4096]{1,0:T(8,128)(2,1)S(1)}, f32[112,1024]{1,0:T(8,128)S(1)}, f32[112,1024]{1,0:T(8,128)S(1)}) custom-call(s32[96]{0:T(128)} %add_bitcast_fusion.code_ref, f32[896]{0:T(1024)} %gain_ref.1, bf16[192,4096]{1,0:T(8,128)(2,1)} %q_hbm.1, bf16[192,4096]{1,0:T(8,128)(2,1)} %g_hbm.1, bf16[8,32,896]{2,1,0:T(8,128)(2,1)} %pool_hbm.1, ...), custom_call_target="tpu_custom_call" | custom-call | tf_op jit(solution)/shard_map/pallas_call | solution.py:652
  96.3 1.1 %copy.15 = bf16[192,4096]{1,0:T(8,128)(2,1)} copy(bf16[192,4096]{1,0:T(8,128)(2,1)S(1)} %get-tuple-element.3) | data formatting | bytes 3145728
  97.5 0.8 copy.16
  98.3 0.8 copy.17
